TPU v7x, 32 devices: a whole 2x2x4 slice. The times are simulated.
32 devices in a mesh: dev: 8 (over z, x), rep: 4 (over y, core).
Axes of the slice: x: 2, y: 2, z: 4, core: 2. Of those that a mesh axis runs over, the one named last changes fastest.
Arguments:
- activations: bfloat16 [4, 64, 64, 512], P('rep', 'dev'), may hold values from -6 to 6
- out_grads: bfloat16 [4, 64, 64, 256], P('rep', 'dev'), may hold values from -6 to 6
- inverse: float32 [8, 2048, 2048], P('dev'), may hold values from -4 to 11, as said below
Outputs:
- whitened: float32 [4, 64, 16384], P('rep', 'dev')
- leverage: float32 [4, 64], P('rep', 'dev')
- new_inverse: float32 [8, 2048, 2048], P('dev', 'rep')
Inputs may be any that keep to these rules, and one draw needn't show every extreme that they name: Each 2048 x 2048 matrix of inverse is symmetric positive definite.
All inputs are finite; a program needn't handle non-finite values.
Results may differ from a plain program's by a relative error of at most 0.0003.
Values sent between devices are 32-bit elements; how exact they have to be, the bound alone decides.
A program may use at most 128 MiB of HBM per device.

v0:
```python
import jax
import jax.numpy as jnp
from jax import lax
from jax.sharding import PartitionSpec as P

KI = 64
KO = 32


def body(activations, out_grads, inverse):
    num_dev = lax.axis_size("dev")
    num_rep = lax.axis_size("rep")
    examples = activations.shape[1]
    tokens = activations.shape[2]
    feat_width = KI * KO
    group_rows = examples * num_dev
    acts_four = activations.reshape(examples, tokens, num_dev, KI)
    grads_four = out_grads.reshape(examples, tokens, num_dev, KO)
    features = jnp.einsum(
        "etmo,etmi->emoi", grads_four, acts_four, preferred_element_type=jnp.float32
    )
    features = features.reshape(examples, num_dev, feat_width) * tokens ** (-0.5)
    moved = lax.all_to_all(features, "dev", split_axis=1, concat_axis=0, tiled=True)
    own_rows = moved[:, 0, :]
    module_inverse = inverse[0]
    whitened = jnp.dot(own_rows, module_inverse, precision=lax.Precision.HIGHEST)
    lev_terms = jnp.sum(own_rows * whitened, axis=1)
    lev_send = lax.psum(lev_terms, "dev") / (num_dev * feat_width)
    all_rows, all_white, all_lev = (
        lax.all_gather(own_rows, "rep", axis=0, tiled=True),
        lax.all_gather(whitened, "rep", axis=0, tiled=True),
        lax.all_gather(lev_send, "rep", axis=0, tiled=True),
    )
    damping = 1.0 + feat_width * all_lev
    capacitance = jnp.dot(all_rows, all_white.T, precision=lax.Precision.HIGHEST) + jnp.diag(
        damping
    )
    cholesky_factor = jnp.linalg.cholesky(capacitance)
    row_count = feat_width // num_rep
    first_row = lax.axis_index("rep") * row_count
    white_block = lax.dynamic_slice_in_dim(all_white, first_row, row_count, 1)
    solved = jax.scipy.linalg.cho_solve((cholesky_factor, True), white_block)
    inverse_rows = lax.dynamic_slice_in_dim(module_inverse, first_row, row_count, 0)
    updated = inverse_rows - jnp.dot(solved.T, all_white, precision=lax.Precision.HIGHEST)
    returned = lax.all_to_all(
        whitened.reshape(num_dev, examples, 1, feat_width),
        "dev",
        split_axis=0,
        concat_axis=2,
        tiled=True,
    )
    whitened_out = returned.reshape(1, examples, num_dev * feat_width)
    lev_first = lax.axis_index("rep") * group_rows + lax.axis_index("dev") * examples
    lev_out = lax.dynamic_slice_in_dim(all_lev, lev_first, examples, 0).reshape(1, examples)
    return (whitened_out, lev_out, updated.reshape(1, row_count, feat_width))


def solution(mesh):
    in_specs = (P("rep", "dev", None, None), P("rep", "dev", None, None), P("dev", None, None))
    out_specs = (P("rep", "dev", None), P("rep", "dev"), P("dev", "rep", None))
    return jax.shard_map(body, mesh=mesh, in_specs=in_specs, out_specs=out_specs, check_vma=False)
```

profile of v0, /device:TPU:0, one launch (start us, length us, event | category | flops | bytes accessed | tf_op | source)
XLA Modules:
  0.0 161.5 jit_solution(12743339337703648658)
XLA Ops:
  7.2 1.2 copy.14
  8.4 1.6 %reshape.57 = bf16[8,64,8,64]{3,2,1,0:T(8,128)(2,1)S(1)} reshape(bf16[1,8,64,512]{3,2,1,0:T(8,128)(2,1)} %param.3) | data formatting | bytes 1048576 | tf_op jit(solution)/shard_map/reshape | solution.py:17
  10.1 0.4 convolution_multiply_fusion
  10.5 0.4 mul.29
  10.9 0.3 copy.16
  11.2 21.7 %all_to_all.30 = f32[8,8,2048]{2,0,1:T(8,128)} all-to-all(f32[8,8,2048]{2,0,1:T(8,128)S(1)} %copy.16), channel_id=1, replica_groups=mesh['dev'=8,'rep'=4] {'dev'}, dimensions={1} | all-to-all | bytes 1048576 | tf_op jit(solution)/shard_map/all_to_all | solution.py:23
  32.9 14.7 %multiply_reduce_fusion = (f32[64]{0:T(128)S(1)}, f32[64,2048]{1,0:T(8,128)}) fusion(f32[8,8,2048]{2,0,1:T(8,128)} %all_to_all.30, f32[1,2048,2048]{2,1,0:T(8,128)} %param.5), kind=kOutput, calls=%fused_computation.14 | convolution fusion | flops 3221487616 | bytes 17826048 | tf_op jit(solution)/shard_map/dot_general | solution.py:26
  47.7 3.6 %all-to-all-start.1 = ((f32[8,8,1,2048]{3,1,2,0:T(8,128)}), f32[8,8,1,2048]{3,1,2,0:T(8,128)S(1)}, u32[]{:S(2)}, u32[]{:S(2)}) async-start(f32[8,8,1,2048]{3,1,2,0:T(8,128)} %bitcast.80), calls=%async_computation.1 | async-start | bytes 1048576 | tf_op jit(solution)/shard_map/all_to_all | solution.py:45
  51.3 0.6 dynamic-slice.4
  52.6 21.9 %psum.7 = f32[64]{0:T(128)S(1)} all-reduce(f32[64]{0:T(128)S(1)} %get-tuple-element.25), channel_id=1, replica_groups=mesh['dev'=8,'rep'=4] {'dev'}, use_global_device_ids=true, to_apply=%region_1.0 | all-reduce | flops 64 | bytes 512 | tf_op jit(solution)/shard_map/psum | solution.py:28
  74.6 5.6 %all-reduce.1 = f32[256]{0:T(256)S(1)} all-reduce(f32[256]{0:T(256)S(1)} %multiply_dynamic-update-slice_fusion), channel_id=1, replica_groups=mesh['dev'=8,'rep'=4] {'rep'}, use_global_device_ids=true, to_apply=%add.1 | all-reduce | flops 256 | bytes 2048
  80.2 0.6 dynamic-slice_bitcast_fusion
  80.8 4.1 %fusion.23 = f32[256,256]{1,0:T(8,128)S(1)} fusion(f32[256,2048]{1,0:T(8,128)} %all-gather.3.cloned.1.call-done, f32[256,2048]{1,0:T(8,128)} %all-gather.5.cloned.1.call-done), kind=kOutput, calls=%fused_computation.51 | convolution fusion | flops 1610612736 | bytes 4456448 | tf_op jit(solution)/shard_map/dot_general | solution.py:35
  85.2 11.7 %cholesky.49 = f32[128,128]{1,0:T(8,128)S(1)} custom-call(f32[128,128]{1,0:T(8,128)S(1)} %cholesky.115), custom_call_target="Cholesky" | custom-call | tf_op jit(solution)/shard_map/jit(cholesky)/cholesky | solution.py:38
  97.0 9.8 %custom-call.18 = f32[1,128,128]{1,2,0:T(8,128)S(1)} custom-call(f32[1,128,128]{2,1,0:T(8,128)S(1)} %get-tuple-element.24), custom_call_target="InvertDiagBlocksLowerTriangular" | custom-call | tf_op jit(solution)/shard_map/jit(cholesky)/cholesky | solution.py:38
  107.0 0.3 convolution_subtract_fusion.2
  107.3 11.8 %cholesky.103 = f32[128,128]{1,0:T(8,128)S(1)} custom-call(f32[128,128]{1,0:T(8,128)S(1)} %convolution_subtract_fusion.2), custom_call_target="Cholesky" | custom-call | tf_op jit(solution)/shard_map/jit(cholesky)/cholesky | solution.py:38
  119.1 0.7 compare_reduce_fusion
  121.1 3.9 %while.1 = (s32[]{:T(128)}, f32[256,256]{1,0:T(8,128)S(1)}, s32[2,2]{1,0:T(2,128)S(1)}, f32[2,128,128]{2,1,0:T(8,128)S(1)}, s32[]{:T(128)}) while((s32[]{:T(128)}, f32[256,256]{1,0:T(8,128)S(1)}, s32[2,2]{1,0:T(2,128)S(1)}, f32[2,128,128]{2,1,0:T(8,128)S(1)}, s32[]{:T(128)}) %tuple.28), condition=%wide.while_cond, body=%wide.while_body.sunk | while | flops 2 | bytes 131189 | solution.py:42
  121.1 0.6 fusion.36
  121.7 1.4 bitcast_dynamic-update-slice_fusion.2
  123.1 0.6 fusion.36
  123.7 1.4 bitcast_dynamic-update-slice_fusion.2
  125.1 19.7 %custom-call.19 = f32[2,128,128]{1,2,0:T(8,128)S(1)} custom-call(f32[2,128,128]{2,1,0:T(8,128)S(1)} %get-tuple-element.10), custom_call_target="InvertDiagBlocksLowerTriangular" | custom-call | tf_op jit(solution)/shard_map/jit(_cho_solve)/triangular_solve | solution.py:42
  144.7 0.4 fusion.7
  145.2 0.4 convolution_subtract_fusion.1
  145.6 0.4 fusion.16
  146.0 0.4 fusion.15
  146.4 0.4 convolution_subtract_fusion
  146.8 0.4 fusion.14
  147.2 6.7 %fusion.2 = f32[1,512,2048]{2,1,0:T(8,128)} fusion(f32[1,2048,2048]{2,1,0:T(8,128)} %param.5, s32[]{:T(128)S(6)} %select_n.20, f32[256,2048]{1,0:T(8,128)S(1)} %copy-done, f32[128,512]{1,0:T(8,128)S(1)} %fusion.15, f32[128,512]{1,0:T(8,128)S(1)} %fusion.14), kind=kOutput, calls=%fused_computation.5 | convolution fusion | flops 3222405120 | bytes 11010052 | tf_op jit(solution)/shard_map/dot_general | solution.py:44
  153.8 0.8 copy.33
  (27 shorter events, 0.9 us)
Async XLA Ops:
  7.2 73.7 %all-gather.3.cloned.1.call-start = ((), (), s32[]{:S(2)}) async-start(), calls=%async_computation.2 | async-start | bytes 2621440 | tf_op jit(solution)/shard_map/all_gather | solution.py:30
  32.9 18.4 %copy-start.1 = (u32[32]{0:T(128)S(1)}, u32[32]{0:T(128)}, u32[]{:S(2)}) copy-start(u32[32]{0:T(128)} %constant.143) | copy-start | bytes 388
  32.9 47.9 %all-gather.5.cloned.1.call-start = ((), (), s32[]{:S(2)}) async-start(), calls=%async_computation.3 | async-start | bytes 2621440 | tf_op jit(solution)/shard_map/all_gather | solution.py:31
  47.7 33.1 %all-to-all-start.1 = ((f32[8,8,1,2048]{3,1,2,0:T(8,128)}), f32[8,8,1,2048]{3,1,2,0:T(8,128)S(1)}, u32[]{:S(2)}, u32[]{:S(2)}) async-start(f32[8,8,1,2048]{3,1,2,0:T(8,128)} %bitcast.80), calls=%async_computation.1 | async-start | bytes 1048576 | tf_op jit(solution)/shard_map/all_to_all | solution.py:45
  84.9 59.8 %copy-start = (f32[256,2048]{1,0:T(8,128)S(1)}, f32[256,2048]{1,0:T(8,128)}, u32[]{:S(2)}) copy-start(f32[256,2048]{1,0:T(8,128)} %all-gather.5.cloned.1.call-done) | copy-start | bytes 6291460
Sparse Core Ops, SparseCore 0:
  33.0 21.6 all-gather.2
  56.8 22.5 all-gather.4
where the time goes:
time: 162 us; the launch traced here: 161 us
  other arithmetic  53.9 us (33%)
  blocking collectives  49.3 us (30%)
  matrix products  28.7 us (18%)
  between operations  16.2 us (10%)
  local copies, waits for them, and re-layouts  9.64 us (6%)
  starting transfers between devices  3.68 us (2%)
    another operation x6, other arithmetic, body(): cholesky_factor = jnp.linalg.cholesky(capacitance)  34 us
    psum x1, blocking collectives, body(): lev_send = lax.psum(lev_terms, 'dev') / (num_dev * feat_width)  21.9 us
    all_to_all x1, blocking collectives, body(): lax.all_to_all(features, 'dev', split_axis=1, concat_axis=0, tiled=True)  21.7 us
    another operation x3, other arithmetic, body(): solved = jax.scipy.linalg.cho_solve((cholesky_factor, True), white_block)  19.7 us
    dot_general x1, matrix products, body(): jnp.dot(own_rows, module_inverse, precision=lax.Precision.HIGHEST)  14.7 us
    dot_general x1, matrix products, body(): jnp.dot(solved.T, all_white, precision=lax.Precision.HIGHEST)  6.68 us
    unnamed x1, blocking collectives  5.63 us
    dot_general x1, matrix products, body(): jnp.dot(all_rows, all_white.T, precision=lax.Precision.HIGHEST)  4.08 us
  transfers between devices with their start and end apart: 3, of which 0 were waited for; matrix products, arithmetic and copies ran while one was open for 10% of the time, Pallas kernels for 0%

commit v1 on v0

v1 whole, which is shorter than its diff:
```python
import functools

import jax
import jax.numpy as jnp
from jax import lax
from jax.experimental import pallas as pl
from jax.experimental.pallas import tpu as pltpu
from jax.sharding import PartitionSpec as P

KI = 64
KO = 32
VMEM_BYTES = 58 * 1024 * 1024
BLOCK = 128
PANEL = 32


def two_terms(value):
    high = value.astype(jnp.bfloat16)
    low = (value - high.astype(jnp.float32)).astype(jnp.bfloat16)
    return high, low


def dot3(left, right, dims):
    left_high, left_low = left
    right_high, right_low = right
    dot = functools.partial(
        lax.dot_general,
        dimension_numbers=(dims, ((), ())),
        preferred_element_type=jnp.float32,
    )
    return dot(left_high, right_high) + (dot(left_high, right_low) + dot(left_low, right_high))


def dot_full(left, right):
    return jnp.dot(
        left, right, precision=lax.Precision.HIGHEST, preferred_element_type=jnp.float32
    )


def gather_kernel(
    num_dev,
    num_rep,
    examples,
    send_ref,
    inverse_ref,
    white_ref,
    cap_ref,
    lev_ref,
    rows,
    columns,
    cols_high,
    cols_low,
    lev_dev,
    lev_rep,
    load_sem,
    own_sem,
    a2a_send,
    a2a_recv,
    row_send,
    row_recv,
    white_send,
    white_recv,
    lev_send,
    lev_recv,
    lrep_send,
    lrep_recv,
):
    dev = lax.axis_index("dev")
    rep = lax.axis_index("rep")
    group = num_dev * examples
    total = num_rep * group
    width = columns.shape[1]
    low_count = 2 if num_rep % 2 == 0 else 1
    high_count = num_rep // low_count
    low = lax.rem(rep, low_count)
    high = rep // low_count
    sibling = high * low_count + (low_count - 1 - low)

    def high_peer(step):
        return lax.rem(high + step, high_count) * low_count + low

    def high_source(step):
        return lax.rem(high + high_count - step, high_count) * low_count + low

    load = pltpu.make_async_copy(
        inverse_ref.at[0, :, pl.ds(pl.multiple_of(rep * width, 128), width)], columns, load_sem
    )
    load.start()

    barrier = pltpu.get_barrier_semaphore()
    for step in range(1, num_dev):
        pl.semaphore_signal(
            barrier, inc=1, device_id={"dev": lax.rem(dev + step, num_dev), "rep": rep}
        )
    for step in range(1, num_rep):
        pl.semaphore_signal(
            barrier, inc=1, device_id={"dev": dev, "rep": lax.rem(rep + step, num_rep)}
        )
    pl.semaphore_wait(barrier, num_dev - 1 + num_rep - 1)

    def row_slice(owner_rep, source):
        return rows.at[pl.ds(pl.multiple_of(owner_rep * group + source * examples, 8), examples)]

    def a2a(step):
        target = lax.rem(dev + step, num_dev)
        return pltpu.make_async_remote_copy(
            src_ref=send_ref.at[target],
            dst_ref=row_slice(rep, dev),
            send_sem=a2a_send.at[step],
            recv_sem=a2a_recv.at[step],
            device_id={"dev": target, "rep": rep},
        )

    own = pltpu.make_async_copy(send_ref.at[dev], row_slice(rep, dev), own_sem)
    own.start()

    def start_a2a(step, carry):
        a2a(step).start()
        return carry

    lax.fori_loop(1, num_dev, start_a2a, 0)

    def pass_on(owner, source, kind, slot, target):
        piece = row_slice(owner, source)
        return pltpu.make_async_remote_copy(
            src_ref=piece,
            dst_ref=piece,
            send_sem=row_send.at[kind, slot],
            recv_sem=row_recv.at[kind, slot],
            device_id={"dev": dev, "rep": target},
        )

    def source_at(step):
        return lax.rem(dev + num_dev - step, num_dev)

    def send_on(step):
        source = source_at(step)
        for far in range(1, high_count):
            pass_on(rep, source, far, step, high_peer(far)).start()
        if low_count == 2:
            pass_on(rep, source, 0, step, sibling).start()

    own.wait()
    send_on(0)
    load.wait()
    high_part, low_part = two_terms(columns[...])
    cols_high[...] = high_part
    cols_low[...] = low_part

    def on_arrival(step, carry):
        a2a(step).wait_recv()
        send_on(step)
        return carry

    lax.fori_loop(1, num_dev, on_arrival, 0)

    def forward(step, carry):
        for far in range(1, high_count):
            pass_on(high_source(far), source_at(step), far, step, rep).wait_recv()
            if low_count == 2:
                pass_on(
                    high_source(far), source_at(step), high_count + far, step, sibling
                ).start()
        return carry

    lax.fori_loop(0, num_dev, forward, 0)

    def finish(step, carry):
        if low_count == 2:
            pass_on(sibling, source_at(step), 0, step, rep).wait_recv()
            for far in range(1, high_count):
                pass_on(sibling, source_at(step), high_count + far, step, rep).wait_recv()
        return carry

    lax.fori_loop(0, num_dev, finish, 0)

    tile = min(256, total)
    own_white = white_ref.at[rep]

    def white_tile(at, carry):
        where = pl.ds(pl.multiple_of(at * tile, tile), tile)
        own_white[where, :] = dot3(
            two_terms(rows[where, :]), (cols_high[...], cols_low[...]), ((1,), (0,))
        )
        return carry

    lax.fori_loop(0, total // tile, white_tile, 0)

    def white_on(owner, part, kind, target):
        piece = white_ref.at[owner, pl.ds(part * group, group)]
        return pltpu.make_async_remote_copy(
            src_ref=piece,
            dst_ref=piece,
            send_sem=white_send.at[kind, part],
            recv_sem=white_recv.at[kind, part],
            device_id={"dev": dev, "rep": target},
        )

    for part in range(num_rep):
        for far in range(1, high_count):
            white_on(rep, part, far, high_peer(far)).start()
        if low_count == 2:
            white_on(rep, part, 0, sibling).start()

    def add_capacitance(block):
        row_block = two_terms(
            rows[:, pl.ds(pl.multiple_of(block * width, 128), width)]
        )
        return dot3(row_block, two_terms(white_ref[block]), ((1,), (1,)))

    diagonal = lax.broadcasted_iota(jnp.int32, (total, total), 0) == lax.broadcasted_iota(
        jnp.int32, (total, total), 1
    )
    cap_ref[...] = add_capacitance(rep)
    own_terms = jnp.sum(jnp.where(diagonal, cap_ref[...], 0.0), axis=0, keepdims=True)
    lev_dev[0] = jnp.broadcast_to(own_terms, (8, total))

    def lev_copy(step):
        return pltpu.make_async_remote_copy(
            src_ref=lev_dev.at[0],
            dst_ref=lev_dev.at[step],
            send_sem=lev_send.at[step],
            recv_sem=lev_recv.at[step],
            device_id={"dev": lax.rem(dev + step, num_dev), "rep": rep},
        )

    def lev_start(step, carry):
        lev_copy(step).start()
        return carry

    lax.fori_loop(1, num_dev, lev_start, 0)

    def lev_wait(step, carry):
        lev_copy(step).wait_recv()
        return carry

    lax.fori_loop(1, num_dev, lev_wait, 0)
    lev_rep[0] = jnp.sum(lev_dev[...], axis=0)

    def lrep_copy(step):
        return pltpu.make_async_remote_copy(
            src_ref=lev_rep.at[0],
            dst_ref=lev_rep.at[step],
            send_sem=lrep_send.at[step],
            recv_sem=lrep_recv.at[step],
            device_id={"dev": dev, "rep": lax.rem(rep + step, num_rep)},
        )

    for step in range(1, num_rep):
        lrep_copy(step).start()

    if low_count == 2:
        for part in range(num_rep):
            white_on(sibling, part, 0, rep).wait_recv()
        cap_ref[...] += add_capacitance(sibling)
    for far in range(1, high_count):
        source = high_source(far)
        for part in range(num_rep):
            white_on(source, part, far, rep).wait_recv()
            if low_count == 2:
                white_on(source, part, high_count + far, sibling).start()
        cap_ref[...] += add_capacitance(source)
    if low_count == 2:
        for far in range(1, high_count):
            source = lax.rem(high + high_count - far, high_count) * 2 + (1 - low)
            for part in range(num_rep):
                white_on(source, part, high_count + far, rep).wait_recv()
            cap_ref[...] += add_capacitance(source)

    for step in range(1, num_rep):
        lrep_copy(step).wait_recv()
    leverage = jnp.sum(lev_rep[...], axis=0) / (num_dev * width * num_rep)
    lev_ref[...] = leverage
    damping = 1.0 + (width * num_rep) * leverage[0:1, :]
    cap_ref[...] = cap_ref[...] + jnp.where(diagonal, damping, 0.0)

    def drain(step, carry):
        a2a(step).wait_send()
        lev_copy(step).wait_send()
        return carry

    lax.fori_loop(1, num_dev, drain, 0)

    def drain_rows(step, carry):
        for kind in range(0 if low_count == 2 else 1, 2 * high_count if low_count == 2 else high_count):
            if kind != high_count:
                pass_on(rep, source_at(step), kind, step, rep).wait_send()
        return carry

    lax.fori_loop(0, num_dev, drain_rows, 0)
    for part in range(num_rep):
        for kind in range(0 if low_count == 2 else 1, 2 * high_count if low_count == 2 else high_count):
            if kind != high_count:
                white_on(rep, part, kind, rep).wait_send()
    for step in range(1, num_rep):
        lrep_copy(step).wait_send()


def invert_block(block_ref):
    lane = lax.broadcasted_iota(jnp.int32, (PANEL, BLOCK), 1)
    row = lax.broadcasted_iota(jnp.int32, (PANEL, BLOCK), 0)
    lane_all = lax.broadcasted_iota(jnp.int32, (BLOCK, BLOCK), 1)
    for first in range(0, BLOCK, PANEL):
        panel = block_ref[first : first + PANEL, :]
        for at in range(PANEL):
            col = first + at
            column = jnp.broadcast_to(panel[:, col : col + 1], (PANEL, BLOCK))
            inverse_pivot = 1.0 / column[at : at + 1, :]
            pivot_row = jnp.where(lane[:1] == col, 1.0, panel[at : at + 1, :]) * inverse_pivot
            panel = jnp.where(
                row == at, pivot_row, jnp.where(lane == col, 0.0, panel) - column * pivot_row
            )
        whole = block_ref[...]
        inside = (lane_all >= first) & (lane_all < first + PANEL)
        block_ref[...] = jnp.where(inside, 0.0, whole) - dot_full(
            whole[:, first : first + PANEL], panel
        )
        block_ref[first : first + PANEL, :] = panel


def update_kernel(rep_ref, cap_ref, white_ref, inverse_ref, out_ref, cap, block, rows, high, low):
    total = cap.shape[0]

    @pl.when(pl.program_id(0) == 0)
    def _():
        cap[...] = cap_ref[...]

        def eliminate(at, carry):
            where = pl.ds(pl.multiple_of(at * BLOCK, BLOCK), BLOCK)
            block[...] = cap[where, where]
            invert_block(block)
            column = cap[:, where]
            cap[:, where] = jnp.zeros((total, BLOCK), jnp.float32)
            rows[...] = dot_full(block[...], cap[where, :])
            rows[:, where] = block[...]
            cap[...] = cap[...] - dot_full(column, rows[...])
            cap[where, :] = rows[...]
            return carry

        lax.fori_loop(0, total // BLOCK, eliminate, 0)
        solved = dot3(
            two_terms(white_ref[rep_ref[0]]), two_terms(cap[...]), ((0,), (0,))
        )
        high_part, low_part = two_terms(solved)
        high[...] = high_part
        low[...] = low_part

    out_ref[0] = inverse_ref[0] - dot3(
        (high[...], low[...]), two_terms(white_ref[pl.program_id(0)]), ((1,), (0,))
    )


def body(activations, out_grads, inverse):
    num_dev = lax.axis_size("dev")
    num_rep = lax.axis_size("rep")
    examples = activations.shape[1]
    tokens = activations.shape[2]
    feat_width = KI * KO
    group_rows = examples * num_dev
    total = group_rows * num_rep
    width = feat_width // num_rep
    acts_four = activations.reshape(examples, tokens, num_dev, KI)
    grads_four = out_grads.reshape(examples, tokens, num_dev, KO)
    features = jnp.einsum(
        "etmo,etmi->emoi", grads_four, acts_four, preferred_element_type=jnp.float32
    )
    features = features.reshape(examples, num_dev, feat_width) * tokens ** (-0.5)
    to_send = features.transpose(1, 0, 2)
    vmem = pl.BlockSpec(memory_space=pltpu.VMEM)
    hbm = pl.BlockSpec(memory_space=pl.ANY)
    dma = pltpu.SemaphoreType.DMA
    all_white, capacitance, all_lev = pl.pallas_call(
        functools.partial(gather_kernel, num_dev, num_rep, examples),
        name="gather_and_whiten",
        out_shape=(
            jax.ShapeDtypeStruct((num_rep, total, width), jnp.float32),
            jax.ShapeDtypeStruct((total, total), jnp.float32),
            jax.ShapeDtypeStruct((8, total), jnp.float32),
        ),
        in_specs=[vmem, hbm],
        out_specs=(vmem, vmem, vmem),
        scratch_shapes=[
            pltpu.VMEM((total, feat_width), jnp.float32),
            pltpu.VMEM((feat_width, width), jnp.float32),
            pltpu.VMEM((feat_width, width), jnp.bfloat16),
            pltpu.VMEM((feat_width, width), jnp.bfloat16),
            pltpu.VMEM((num_dev, 8, total), jnp.float32),
            pltpu.VMEM((num_rep, 8, total), jnp.float32),
            dma,
            dma,
            dma((num_dev,)),
            dma((num_dev,)),
            dma((num_rep + 1, num_dev)),
            dma((num_rep + 1, num_dev)),
            dma((num_rep + 1, num_rep)),
            dma((num_rep + 1, num_rep)),
            dma((num_dev,)),
            dma((num_dev,)),
            dma((num_rep,)),
            dma((num_rep,)),
        ],
        compiler_params=pltpu.CompilerParams(
            collective_id=0, has_side_effects=True, vmem_limit_bytes=VMEM_BYTES
        ),
    )(to_send, inverse)

    rep = lax.axis_index("rep")
    first_group = rep * group_rows
    own_white = lax.dynamic_slice_in_dim(all_white, first_group, group_rows, 1)
    own_white = own_white.reshape(num_rep, num_dev, examples, width)
    own_white = own_white.transpose(1, 2, 0, 3).reshape(num_dev, examples, 1, feat_width)
    returned = lax.all_to_all(own_white, "dev", split_axis=0, concat_axis=2, tiled=True)
    whitened_out = returned.reshape(1, examples, num_dev * feat_width)

    updated = pl.pallas_call(
        update_kernel,
        name="solve_and_update",
        grid_spec=pltpu.PrefetchScalarGridSpec(
            num_scalar_prefetch=1,
            grid=(num_rep,),
            in_specs=[
                pl.BlockSpec((total, total), lambda c, r: (0, 0)),
                pl.BlockSpec((num_rep, total, width), lambda c, r: (0, 0, 0)),
                pl.BlockSpec((1, width, width), lambda c, r: (0, r[0], c)),
            ],
            out_specs=pl.BlockSpec((1, width, width), lambda c, r: (0, 0, c)),
            scratch_shapes=[
                pltpu.VMEM((total, total), jnp.float32),
                pltpu.VMEM((BLOCK, BLOCK), jnp.float32),
                pltpu.VMEM((BLOCK, total), jnp.float32),
                pltpu.VMEM((width, total), jnp.bfloat16),
                pltpu.VMEM((width, total), jnp.bfloat16),
            ],
        ),
        out_shape=jax.ShapeDtypeStruct((1, width, feat_width), jnp.float32),
        compiler_params=pltpu.CompilerParams(vmem_limit_bytes=VMEM_BYTES),
        cost_estimate=pl.CostEstimate(
            flops=8 * total * width * feat_width, bytes_accessed=16 * total * feat_width, transcendentals=0
        ),
    )(jnp.reshape(rep, (1,)).astype(jnp.int32), capacitance, all_white, inverse)

    lev_first = first_group + lax.axis_index("dev") * examples
    lev_out = lax.dynamic_slice_in_dim(all_lev[0], lev_first, examples, 0).reshape(1, examples)
    return (whitened_out, lev_out, updated)


def solution(mesh):
    in_specs = (P("rep", "dev", None, None), P("rep", "dev", None, None), P("dev", None, None))
    out_specs = (P("rep", "dev", None), P("rep", "dev"), P("dev", "rep", None))
    return jax.shard_map(body, mesh=mesh, in_specs=in_specs, out_specs=out_specs, check_vma=False)
```

time: 162 us -> 91.3 us (0.56)
  Pallas kernels: 0 us -> 73.8 us
  other arithmetic: 53.9 us -> 0 us
  blocking collectives: 49.3 us -> 0 us
  matrix products: 28.7 us -> 0.39 us
  between operations: 16.2 us -> 0.67 us
  starting transfers between devices: 3.68 us -> 7.03 us
    pallas_call x0 -> x2, Pallas kernels: none -> 73.8 us  [the longest x1 42.4 us: body(): pl.pallas_call(functools.partial(gather_kernel, num_dev, num_rep, example...]
    another operation x9 -> x0, other arithmetic: 53.7 us -> none  [the longest x6 34 us: body(): cholesky_factor = jnp.linalg.cholesky(capacitance)]
    dot_general x3 -> x0, matrix products: 25.5 us -> none  [the longest x1 14.7 us: body(): jnp.dot(own_rows, module_inverse, precision=lax.Precision.HIGHEST)]
    psum x1 -> x0, blocking collectives: 21.9 us -> none  [body(): lev_send = lax.psum(lev_terms, 'dev') / (num_dev * feat_width)]
    all_to_all x1 -> x0, blocking collectives: 21.7 us -> none  [body(): lax.all_to_all(features, 'dev', split_axis=1, concat_axis=0, tiled=True)]
    unnamed x1 -> x0, blocking collectives: 5.63 us -> none
    another operation x9 -> x0, local copies, waits for them, and re-layouts: 3.99 us -> none
    all_to_all x1, starting transfers between devices: 3.6 us -> 7.03 us  [body(): lax.all_to_all(own_white, 'dev', split_axis=0, concat_axis=2, tiled=True)]
  transfers between devices with their start and end apart: 3 -> 1, of which waited for: 0 -> 0; matrix products, arithmetic and copies ran while one was open for 10% -> 1% of each run, Pallas kernels for 0% -> 35%
where the time goes in v1:
time: 91.3 us; the launch traced here: 90.9 us
  Pallas kernels  73.8 us (81%)
  local copies, waits for them, and re-layouts  9 us (10%)
  starting transfers between devices  7.03 us (8%)
    pallas_call x1, Pallas kernels, body(): pl.pallas_call(functools.partial(gather_kernel, num_dev, num_rep, example...  42.4 us
    pallas_call x1, Pallas kernels, body(): pl.pallas_call(update_kernel, name='solve_and_update', grid_spec=pltpu.Pr...  31.4 us
    all_to_all x1, starting transfers between devices, body(): lax.all_to_all(own_white, 'dev', split_axis=0, concat_axis=2, tiled=True)  7.03 us
    unnamed x2, local copies, waits for them, and re-layouts  2.02 us
  transfers between devices with their start and end apart: 1, of which 0 were waited for; matrix products, arithmetic and copies ran while one was open for 1% of the time, Pallas kernels for 35%

profile of v1, /device:TPU:0, one launch (start us, length us, event | category | flops | bytes accessed | tf_op | source)
XLA Modules:
  0.0 90.9 jit_solution(6314633317399217440)
XLA Ops:
  0.6 1.2 %copy.16 = bf16[1,8,64,256]{2,3,1,0:T(8,128)(2,1)S(1)} copy(bf16[1,8,64,256]{3,2,1,0:T(8,128)(2,1)} %param.4) | data formatting | bytes 524288 | tf_op args[1]
  1.9 1.6 %reshape.32 = bf16[8,64,8,64]{3,2,1,0:T(8,128)(2,1)S(1)} reshape(bf16[1,8,64,512]{3,2,1,0:T(8,128)(2,1)} %param.3) | data formatting | bytes 1048576 | tf_op jit(solution)/shard_map/reshape | solution.py:362
  3.5 0.4 convolution_multiply_fusion
  3.9 0.4 reshape.37
  4.3 1.1 %copy.25 = f32[8,8,2048]{2,0,1:T(8,128)} copy(f32[8,8,2048]{2,1,0:T(8,128)S(1)} %reshape.37) | data formatting | bytes 1048576 | tf_op jit(solution)/shard_map/mul | solution.py:367
  5.4 42.4 %gather_and_whiten.1 = (f32[4,256,512]{2,1,0:T(8,128)}, f32[256,256]{1,0:T(8,128)}, f32[8,256]{1,0:T(8,128)}) custom-call(f32[8,8,2048]{2,1,0:T(8,128)} %bitcast.20, f32[1,2048,2048]{2,1,0:T(8,128)} %inverse_ref.3), custom_call_target="tpu_custom_call" | custom-call | tf_op jit(solution)/shard_map/gather_and_whiten/pallas_call | solution.py:372
  47.8 1.1 %dynamic-slice_bitcast_fusion = f32[8,8,4,512]{3,1,0,2:T(8,128)S(1)} fusion(f32[4,256,512]{2,1,0:T(8,128)} %get-tuple-element.6.white_ref, s32[]{:T(128)S(6)} %select_n.6), kind=kLoop, calls=%fused_computation.3 | loop fusion | bytes 1048580 | tf_op jit(solution)/shard_map/transpose | solution.py:411
  48.9 0.3 copy.19
  49.2 1.2 %reshape.34 = f32[8,8,1,2048]{3,1,0,2:T(8,128)} reshape(f32[8,8,4,512]{3,2,1,0:T(4,128)S(1)} %copy.19) | data formatting | bytes 1048576 | tf_op jit(solution)/shard_map/reshape | solution.py:411
  50.4 7.0 %all-to-all-start = ((f32[8,8,1,2048]{3,1,2,0:T(8,128)}), f32[8,8,1,2048]{3,1,2,0:T(8,128)S(1)}, u32[]{:S(2)}, u32[]{:S(2)}) async-start(f32[8,8,1,2048]{3,1,2,0:T(8,128)} %bitcast.4), calls=%async_computation | async-start | bytes 1048576 | tf_op jit(solution)/shard_map/all_to_all | solution.py:412
  57.4 0.7 slice.3
  58.1 0.6 constant_dynamic-slice_fusion
  58.7 31.4 %solve_and_update.1 = f32[1,512,2048]{2,1,0:T(8,128)} custom-call(s32[1]{0:T(128)} %bitcast.8.rep_ref, f32[256,256]{1,0:T(8,128)} %get-tuple-element.8.cap_ref, f32[4,256,512]{2,1,0:T(8,128)} %get-tuple-element.6.white_ref, f32[1,2048,2048]{2,1,0:T(8,128)} %inverse_ref.3), custom_call_target="tpu_custom_call" | custom-call | flops 2147483648 | bytes 8388608 | tf_op jit(solution)/shard_map/solve_and_update/pallas_call | solution.py:415
  90.1 0.0 all-to-all-done
  90.1 0.8 copy.27
Async XLA Ops:
  50.4 39.7 %all-to-all-start = ((f32[8,8,1,2048]{3,1,2,0:T(8,128)}), f32[8,8,1,2048]{3,1,2,0:T(8,128)S(1)}, u32[]{:S(2)}, u32[]{:S(2)}) async-start(f32[8,8,1,2048]{3,1,2,0:T(8,128)} %bitcast.4), calls=%async_computation | async-start | bytes 1048576 | tf_op jit(solution)/shard_map/all_to_all | solution.py:412

commit v2 on v1

--- a/solution.py
+++ b/solution.py
@@ -12,6 +12,7 @@
 VMEM_BYTES = 58 * 1024 * 1024
 BLOCK = 128
 PANEL = 32
+ROWS = 8
 
 
 def two_terms(value):
@@ -31,10 +32,8 @@
     return dot(left_high, right_high) + (dot(left_high, right_low) + dot(left_low, right_high))
 
 
-def dot_full(left, right):
-    return jnp.dot(
-        left, right, precision=lax.Precision.HIGHEST, preferred_element_type=jnp.float32
-    )
+def dot_terms(left, right):
+    return dot3(two_terms(left), two_terms(right), ((1,), (0,)))
 
 
 def gather_kernel(
@@ -44,14 +43,22 @@
     send_ref,
     inverse_ref,
     white_ref,
-    cap_ref,
+    high_ref,
+    low_ref,
     lev_ref,
+    back_ref,
     rows,
     columns,
     cols_high,
     cols_low,
     lev_dev,
     lev_rep,
+    partial,
+    landed,
+    cap,
+    work,
+    block,
+    block_rows,
     load_sem,
     own_sem,
     a2a_send,
@@ -64,6 +71,13 @@
     lev_recv,
     lrep_send,
     lrep_recv,
+    sum_send,
+    sum_recv,
+    share_send,
+    share_recv,
+    back_send,
+    back_recv,
+    back_own,
 ):
     dev = lax.axis_index("dev")
     rep = lax.axis_index("rep")
@@ -196,23 +210,46 @@
             device_id={"dev": dev, "rep": target},
         )
 
-    for part in range(num_rep):
-        for far in range(1, high_count):
-            white_on(rep, part, far, high_peer(far)).start()
-        if low_count == 2:
+    if low_count == 2:
+        for part in range(num_rep):
             white_on(rep, part, 0, sibling).start()
 
-    def add_capacitance(block):
-        row_block = two_terms(
-            rows[:, pl.ds(pl.multiple_of(block * width, 128), width)]
-        )
-        return dot3(row_block, two_terms(white_ref[block]), ((1,), (1,)))
+    partial[...] = dot3(
+        two_terms(rows[:, pl.ds(pl.multiple_of(rep * width, 128), width)]),
+        two_terms(white_ref[rep]),
+        ((1,), (1,)),
+    )
+
+    def group_rows(ref, owner):
+        return ref.at[pl.ds(pl.multiple_of(owner * group, 8), group)]
+
+    def sum_copy(step):
+        target = lax.rem(rep + step, num_rep)
+        return pltpu.make_async_remote_copy(
+            src_ref=group_rows(partial, target),
+            dst_ref=landed.at[step],
+            send_sem=sum_send.at[step],
+            recv_sem=sum_recv.at[step],
+            device_id={"dev": dev, "rep": target},
+        )
+
+    def share_copy(step):
+        piece = group_rows(cap, rep)
+        return pltpu.make_async_remote_copy(
+            src_ref=piece,
+            dst_ref=piece,
+            send_sem=share_send.at[step],
+            recv_sem=share_recv.at[step],
+            device_id={"dev": dev, "rep": lax.rem(rep + step, num_rep)},
+        )
+
+    for step in range(1, num_rep):
+        sum_copy(step).start()
 
     diagonal = lax.broadcasted_iota(jnp.int32, (total, total), 0) == lax.broadcasted_iota(
         jnp.int32, (total, total), 1
     )
-    cap_ref[...] = add_capacitance(rep)
-    own_terms = jnp.sum(jnp.where(diagonal, cap_ref[...], 0.0), axis=0, keepdims=True)
+    own_terms = jnp.sum(jnp.where(diagonal, partial[...], 0.0), axis=0, keepdims=True)
     lev_dev[0] = jnp.broadcast_to(own_terms, (8, total))
 
     def lev_copy(step):
@@ -230,6 +267,14 @@
 
     lax.fori_loop(1, num_dev, lev_start, 0)
 
+    total_rows = partial[pl.ds(pl.multiple_of(rep * group, 8), group), :]
+    for step in range(1, num_rep):
+        sum_copy(step).wait_recv()
+        total_rows = total_rows + landed[step]
+    cap[pl.ds(pl.multiple_of(rep * group, 8), group), :] = total_rows
+    for step in range(1, num_rep):
+        share_copy(step).start()
+
     def lev_wait(step, carry):
         lev_copy(step).wait_recv()
         return carry
@@ -248,31 +293,105 @@
 
     for step in range(1, num_rep):
         lrep_copy(step).start()
-
+    for step in range(1, num_rep):
+        lrep_copy(step).wait_recv()
+    for step in range(1, num_rep):
+        share_copy(step).wait_recv()
+
+    def part_order(target):
+        if low_count == 2:
+            first = target - lax.rem(target, 2)
+            other = first + 1 - lax.rem(target, 2)
+            return [target, other] + [
+                lax.rem(first + at, num_rep) for at in range(2, num_rep)
+            ]
+        return [lax.rem(target + at, num_rep) for at in range(num_rep)]
+
+    for far in range(1, high_count):
+        for part in part_order(high_peer(far)):
+            white_on(rep, part, far, high_peer(far)).start()
+
+    leverage = jnp.sum(lev_rep[...], axis=0) / (num_dev * width * num_rep)
+    lev_ref[...] = leverage
+    damping = 1.0 + (width * num_rep) * leverage[0:1, :]
+    work[...] = cap[...] + jnp.where(diagonal, damping, 0.0)
+
+    def back_copy(column_block, slot, step):
+        target = lax.rem(dev + step, num_dev)
+        first_row = pl.multiple_of(rep * group + target * examples, 8)
+        first_column = pl.multiple_of((dev * num_rep + column_block) * width, 128)
+        return pltpu.make_async_remote_copy(
+            src_ref=white_ref.at[column_block, pl.ds(first_row, examples)],
+            dst_ref=back_ref.at[:, pl.ds(first_column, width)],
+            send_sem=back_send.at[slot, step],
+            recv_sem=back_recv.at[slot, step],
+            device_id={"dev": target, "rep": rep},
+        )
+
+    def back_local(column_block, slot):
+        first_row = pl.multiple_of(rep * group + dev * examples, 8)
+        first_column = pl.multiple_of((dev * num_rep + column_block) * width, 128)
+        return pltpu.make_async_copy(
+            white_ref.at[column_block, pl.ds(first_row, examples)],
+            back_ref.at[:, pl.ds(first_column, width)],
+            back_own.at[slot],
+        )
+
+    def send_back(column_block, slot):
+        def start_back(step, carry):
+            back_copy(column_block, slot, step).start()
+            return carry
+
+        lax.fori_loop(1, num_dev, start_back, 0)
+        back_local(column_block, slot).start()
+
+    blocks = [(rep, 0)]
+    send_back(rep, 0)
     if low_count == 2:
         for part in range(num_rep):
             white_on(sibling, part, 0, rep).wait_recv()
-        cap_ref[...] += add_capacitance(sibling)
+        blocks.append((sibling, 1))
+        send_back(sibling, 1)
+
+    def pass_white(far, places):
+        source = high_source(far)
+        order = part_order(rep)
+        for place in places:
+            white_on(source, order[place], far, rep).wait_recv()
+            if low_count == 2:
+                white_on(source, order[place], high_count + far, sibling).start()
+
+    early = min(2, num_rep)
+    block_count = total // BLOCK
+    eliminate_blocks(0, block_count // 2, work, block, block_rows)
     for far in range(1, high_count):
-        source = high_source(far)
-        for part in range(num_rep):
-            white_on(source, part, far, rep).wait_recv()
-            if low_count == 2:
-                white_on(source, part, high_count + far, sibling).start()
-        cap_ref[...] += add_capacitance(source)
+        pass_white(far, range(early))
+        blocks.append((high_source(far), low_count * far))
+        send_back(high_source(far), low_count * far)
+    eliminate_blocks(block_count // 2, block_count, work, block, block_rows)
+    for far in range(1, high_count):
+        pass_white(far, range(early, num_rep))
     if low_count == 2:
         for far in range(1, high_count):
             source = lax.rem(high + high_count - far, high_count) * 2 + (1 - low)
             for part in range(num_rep):
                 white_on(source, part, high_count + far, rep).wait_recv()
-            cap_ref[...] += add_capacitance(source)
-
-    for step in range(1, num_rep):
-        lrep_copy(step).wait_recv()
-    leverage = jnp.sum(lev_rep[...], axis=0) / (num_dev * width * num_rep)
-    lev_ref[...] = leverage
-    damping = 1.0 + (width * num_rep) * leverage[0:1, :]
-    cap_ref[...] = cap_ref[...] + jnp.where(diagonal, damping, 0.0)
+            blocks.append((source, 2 * far + 1))
+            send_back(source, 2 * far + 1)
+
+    solved = dot3(two_terms(white_ref[rep]), two_terms(work[...]), ((0,), (0,)))
+    high_part, low_part = two_terms(solved)
+    high_ref[...] = high_part
+    low_ref[...] = low_part
+
+    for column_block, slot in blocks:
+
+        def back_wait(step, carry, column_block=column_block, slot=slot):
+            back_copy(column_block, slot, step).wait()
+            return carry
+
+        lax.fori_loop(1, num_dev, back_wait, 0)
+        back_local(column_block, slot).wait()
 
     def drain(step, carry):
         a2a(step).wait_send()
@@ -294,59 +413,82 @@
                 white_on(rep, part, kind, rep).wait_send()
     for step in range(1, num_rep):
         lrep_copy(step).wait_send()
+        sum_copy(step).wait_send()
+        share_copy(step).wait_send()
 
 
 def invert_block(block_ref):
-    lane = lax.broadcasted_iota(jnp.int32, (PANEL, BLOCK), 1)
-    row = lax.broadcasted_iota(jnp.int32, (PANEL, BLOCK), 0)
+    lane = lax.broadcasted_iota(jnp.int32, (ROWS, BLOCK), 1)
+    row = lax.broadcasted_iota(jnp.int32, (ROWS, BLOCK), 0)
     lane_all = lax.broadcasted_iota(jnp.int32, (BLOCK, BLOCK), 1)
+
+    def spread(value, col):
+        return jnp.broadcast_to(value[:, col : col + 1], (ROWS, BLOCK))
+
     for first in range(0, BLOCK, PANEL):
-        panel = block_ref[first : first + PANEL, :]
-        for at in range(PANEL):
-            col = first + at
-            column = jnp.broadcast_to(panel[:, col : col + 1], (PANEL, BLOCK))
-            inverse_pivot = 1.0 / column[at : at + 1, :]
-            pivot_row = jnp.where(lane[:1] == col, 1.0, panel[at : at + 1, :]) * inverse_pivot
-            panel = jnp.where(
-                row == at, pivot_row, jnp.where(lane == col, 0.0, panel) - column * pivot_row
-            )
+        panel = [block_ref[at : at + ROWS, :] for at in range(first, first + PANEL, ROWS)]
+        for part in range(PANEL // ROWS):
+            start = first + part * ROWS
+            pivots = panel[part]
+            columns = [spread(pivots, start + at) for at in range(ROWS)]
+            others = {
+                other: [spread(panel[other], start + at) for at in range(ROWS)]
+                for other in range(PANEL // ROWS)
+                if other != part
+            }
+            for at in range(ROWS):
+                column = columns[at]
+                inverse_pivot = 1.0 / column[at : at + 1, :]
+                for later in range(at + 1, ROWS):
+                    scaled = columns[later][at : at + 1, :] * inverse_pivot
+                    columns[later] = jnp.where(
+                        row == at, scaled, columns[later] - column * scaled
+                    )
+                pivot_row = (
+                    jnp.where(lane[:1] == start + at, 1.0, pivots[at : at + 1, :])
+                    * inverse_pivot
+                )
+                pivots = jnp.where(
+                    row == at,
+                    pivot_row,
+                    jnp.where(lane == start + at, 0.0, pivots) - column * pivot_row,
+                )
+            panel[part] = pivots
+            for other, spreads in others.items():
+                value = jnp.where((lane >= start) & (lane < start + ROWS), 0.0, panel[other])
+                for at in range(ROWS):
+                    value = value - spreads[at] * pivots[at : at + 1, :]
+                panel[other] = value
+        panel = jnp.concatenate(panel, axis=0)
         whole = block_ref[...]
         inside = (lane_all >= first) & (lane_all < first + PANEL)
-        block_ref[...] = jnp.where(inside, 0.0, whole) - dot_full(
+        block_ref[...] = jnp.where(inside, 0.0, whole) - dot_terms(
             whole[:, first : first + PANEL], panel
         )
         block_ref[first : first + PANEL, :] = panel
 
 
-def update_kernel(rep_ref, cap_ref, white_ref, inverse_ref, out_ref, cap, block, rows, high, low):
+def eliminate_blocks(begin, end, cap, block, rows):
     total = cap.shape[0]
 
-    @pl.when(pl.program_id(0) == 0)
-    def _():
-        cap[...] = cap_ref[...]
-
-        def eliminate(at, carry):
-            where = pl.ds(pl.multiple_of(at * BLOCK, BLOCK), BLOCK)
-            block[...] = cap[where, where]
-            invert_block(block)
-            column = cap[:, where]
-            cap[:, where] = jnp.zeros((total, BLOCK), jnp.float32)
-            rows[...] = dot_full(block[...], cap[where, :])
-            rows[:, where] = block[...]
-            cap[...] = cap[...] - dot_full(column, rows[...])
-            cap[where, :] = rows[...]
-            return carry
-
-        lax.fori_loop(0, total // BLOCK, eliminate, 0)
-        solved = dot3(
-            two_terms(white_ref[rep_ref[0]]), two_terms(cap[...]), ((0,), (0,))
-        )
-        high_part, low_part = two_terms(solved)
-        high[...] = high_part
-        low[...] = low_part
-
+    def eliminate(at, carry):
+        where = pl.ds(pl.multiple_of(at * BLOCK, BLOCK), BLOCK)
+        block[...] = cap[where, where]
+        invert_block(block)
+        column = cap[:, where]
+        cap[:, where] = jnp.zeros((total, BLOCK), jnp.float32)
+        rows[...] = dot_terms(block[...], cap[where, :])
+        rows[:, where] = block[...]
+        cap[...] = cap[...] - dot_terms(column, rows[...])
+        cap[where, :] = rows[...]
+        return carry
+
+    lax.fori_loop(begin, end, eliminate, 0)
+
+
+def update_kernel(rep_ref, high_ref, low_ref, white_ref, inverse_ref, out_ref):
     out_ref[0] = inverse_ref[0] - dot3(
-        (high[...], low[...]), two_terms(white_ref[pl.program_id(0)]), ((1,), (0,))
+        (high_ref[...], low_ref[...]), two_terms(white_ref[0]), ((1,), (0,))
     )
 
 
@@ -369,16 +511,18 @@
     vmem = pl.BlockSpec(memory_space=pltpu.VMEM)
     hbm = pl.BlockSpec(memory_space=pl.ANY)
     dma = pltpu.SemaphoreType.DMA
-    all_white, capacitance, all_lev = pl.pallas_call(
+    all_white, solved_high, solved_low, all_lev, returned = pl.pallas_call(
         functools.partial(gather_kernel, num_dev, num_rep, examples),
-        name="gather_and_whiten",
+        name="gather_whiten_solve",
         out_shape=(
             jax.ShapeDtypeStruct((num_rep, total, width), jnp.float32),
-            jax.ShapeDtypeStruct((total, total), jnp.float32),
+            jax.ShapeDtypeStruct((width, total), jnp.bfloat16),
+            jax.ShapeDtypeStruct((width, total), jnp.bfloat16),
             jax.ShapeDtypeStruct((8, total), jnp.float32),
+            jax.ShapeDtypeStruct((examples, num_dev * feat_width), jnp.float32),
         ),
         in_specs=[vmem, hbm],
-        out_specs=(vmem, vmem, vmem),
+        out_specs=(vmem, vmem, vmem, vmem, hbm),
         scratch_shapes=[
             pltpu.VMEM((total, feat_width), jnp.float32),
             pltpu.VMEM((feat_width, width), jnp.float32),
@@ -386,6 +530,12 @@
             pltpu.VMEM((feat_width, width), jnp.bfloat16),
             pltpu.VMEM((num_dev, 8, total), jnp.float32),
             pltpu.VMEM((num_rep, 8, total), jnp.float32),
+            pltpu.VMEM((total, total), jnp.float32),
+            pltpu.VMEM((num_rep, group_rows, total), jnp.float32),
+            pltpu.VMEM((total, total), jnp.float32),
+            pltpu.VMEM((total, total), jnp.float32),
+            pltpu.VMEM((BLOCK, BLOCK), jnp.float32),
+            pltpu.VMEM((BLOCK, total), jnp.float32),
             dma,
             dma,
             dma((num_dev,)),
@@ -398,6 +548,13 @@
             dma((num_dev,)),
             dma((num_rep,)),
             dma((num_rep,)),
+            dma((num_rep,)),
+            dma((num_rep,)),
+            dma((num_rep,)),
+            dma((num_rep,)),
+            dma((num_rep, num_dev)),
+            dma((num_rep, num_dev)),
+            dma((num_rep,)),
         ],
         compiler_params=pltpu.CompilerParams(
             collective_id=0, has_side_effects=True, vmem_limit_bytes=VMEM_BYTES
@@ -405,43 +562,32 @@
     )(to_send, inverse)
 
     rep = lax.axis_index("rep")
-    first_group = rep * group_rows
-    own_white = lax.dynamic_slice_in_dim(all_white, first_group, group_rows, 1)
-    own_white = own_white.reshape(num_rep, num_dev, examples, width)
-    own_white = own_white.transpose(1, 2, 0, 3).reshape(num_dev, examples, 1, feat_width)
-    returned = lax.all_to_all(own_white, "dev", split_axis=0, concat_axis=2, tiled=True)
-    whitened_out = returned.reshape(1, examples, num_dev * feat_width)
-
     updated = pl.pallas_call(
         update_kernel,
-        name="solve_and_update",
+        name="update",
         grid_spec=pltpu.PrefetchScalarGridSpec(
             num_scalar_prefetch=1,
             grid=(num_rep,),
             in_specs=[
-                pl.BlockSpec((total, total), lambda c, r: (0, 0)),
-                pl.BlockSpec((num_rep, total, width), lambda c, r: (0, 0, 0)),
+                pl.BlockSpec((width, total), lambda c, r: (0, 0)),
+                pl.BlockSpec((width, total), lambda c, r: (0, 0)),
+                pl.BlockSpec((1, total, width), lambda c, r: (c, 0, 0)),
                 pl.BlockSpec((1, width, width), lambda c, r: (0, r[0], c)),
             ],
             out_specs=pl.BlockSpec((1, width, width), lambda c, r: (0, 0, c)),
-            scratch_shapes=[
-                pltpu.VMEM((total, total), jnp.float32),
-                pltpu.VMEM((BLOCK, BLOCK), jnp.float32),
-                pltpu.VMEM((BLOCK, total), jnp.float32),
-                pltpu.VMEM((width, total), jnp.bfloat16),
-                pltpu.VMEM((width, total), jnp.bfloat16),
-            ],
         ),
         out_shape=jax.ShapeDtypeStruct((1, width, feat_width), jnp.float32),
         compiler_params=pltpu.CompilerParams(vmem_limit_bytes=VMEM_BYTES),
         cost_estimate=pl.CostEstimate(
-            flops=8 * total * width * feat_width, bytes_accessed=16 * total * feat_width, transcendentals=0
+            flops=6 * total * width * feat_width,
+            bytes_accessed=12 * width * feat_width,
+            transcendentals=0,
         ),
-    )(jnp.reshape(rep, (1,)).astype(jnp.int32), capacitance, all_white, inverse)
-
-    lev_first = first_group + lax.axis_index("dev") * examples
+    )(jnp.reshape(rep, (1,)).astype(jnp.int32), solved_high, solved_low, all_white, inverse)
+
+    lev_first = rep * group_rows + lax.axis_index("dev") * examples
     lev_out = lax.dynamic_slice_in_dim(all_lev[0], lev_first, examples, 0).reshape(1, examples)
-    return (whitened_out, lev_out, updated)
+    return (returned.reshape(1, examples, num_dev * feat_width), lev_out, updated)
 
 
 def solution(mesh):

time: 91.3 us -> 74.7 us (0.82)
  starting transfers between devices: 7.03 us -> 0 us
  Pallas kernels: 73.8 us -> 67 us
  local copies, waits for them, and re-layouts: 9 us -> 6.42 us
    pallas_call x1, Pallas kernels: 31.4 us -> 6.48 us  [body(): pl.pallas_call(update_kernel, name='update', grid_spec=pltpu.PrefetchScal...]
    pallas_call x1, Pallas kernels: 42.4 us -> 60.5 us  [body(): pl.pallas_call(functools.partial(gather_kernel, num_dev, num_rep, example...]
    all_to_all x1 -> x0, starting transfers between devices: 7.03 us -> none  [body(): lax.all_to_all(own_white, 'dev', split_axis=0, concat_axis=2, tiled=True)]
    transpose x2 -> x0, local copies, waits for them, and re-layouts: 1.43 us -> none  [body(): own_white.transpose(1, 2, 0, 3).reshape(num_dev, examples, 1, feat_width)]
    reshape x1 -> x0, local copies, waits for them, and re-layouts: 1.15 us -> none  [body(): own_white.transpose(1, 2, 0, 3).reshape(num_dev, examples, 1, feat_width)]
    unnamed x2 -> x4, local copies, waits for them, and re-layouts: 2.02 us -> 2.02 us
  transfers between devices with their start and end apart: 1 -> 0, of which waited for: 0 -> 0; matrix products, arithmetic and copies ran while one was open for 1% -> 0% of each run, Pallas kernels for 35% -> 0%
where the time goes in v2:
time: 74.7 us; the launch traced here: 74.4 us
  Pallas kernels  67 us (90%)
  local copies, waits for them, and re-layouts  6.42 us (9%)
    pallas_call x1, Pallas kernels, body(): pl.pallas_call(functools.partial(gather_kernel, num_dev, num_rep, example...  60.5 us
    pallas_call x1, Pallas kernels, body(): pl.pallas_call(update_kernel, name='update', grid_spec=pltpu.PrefetchScal...  6.48 us
    unnamed x4, local copies, waits for them, and re-layouts  2.02 us
    reshape x1, local copies, waits for them, and re-layouts, body(): acts_four = activations.reshape(examples, tokens, num_dev, KI)  1.65 us

profile of v2, /device:TPU:0, one launch (start us, length us, event | category | flops | bytes accessed | tf_op | source)
XLA Modules:
  0.0 74.4 jit_solution(10791384029328142081)
XLA Ops:
  0.6 1.2 %copy.9 = bf16[1,8,64,256]{2,3,1,0:T(8,128)(2,1)S(1)} copy(bf16[1,8,64,256]{3,2,1,0:T(8,128)(2,1)} %param.4) | data formatting | bytes 524288 | tf_op args[1]
  1.9 1.6 %reshape.25 = bf16[8,64,8,64]{3,2,1,0:T(8,128)(2,1)S(1)} reshape(bf16[1,8,64,512]{3,2,1,0:T(8,128)(2,1)} %param.3) | data formatting | bytes 1048576 | tf_op jit(solution)/shard_map/reshape | solution.py:504
  3.5 0.4 convolution_multiply_fusion
  3.9 0.4 reshape.28
  4.3 1.1 %copy.16 = f32[8,8,2048]{2,0,1:T(8,128)} copy(f32[8,8,2048]{2,1,0:T(8,128)S(1)} %reshape.28) | data formatting | bytes 1048576 | tf_op jit(solution)/shard_map/mul | solution.py:509
  5.4 60.5 %gather_whiten_solve.1 = (f32[4,256,512]{2,1,0:T(8,128)}, bf16[512,256]{1,0:T(8,128)(2,1)}, bf16[512,256]{1,0:T(8,128)(2,1)}, f32[8,256]{1,0:T(8,128)}, f32[8,16384]{1,0:T(8,128)}) custom-call(f32[8,8,2048]{2,1,0:T(8,128)} %bitcast.11, f32[1,2048,2048]{2,1,0:T(8,128)} %inverse_ref.3), custom_call_target="tpu_custom_call" | custom-call | tf_op jit(solution)/shard_map/gather_whiten_solve/pallas_call | solution.py:514
  65.9 0.7 slice.3
  66.6 0.6 constant_dynamic-slice_fusion
  67.2 0.0 copy-start
  67.2 6.5 %update.1 = f32[1,512,2048]{2,1,0:T(8,128)} custom-call(s32[1]{0:T(128)} %bitcast.3.rep_ref, bf16[512,256]{1,0:T(8,128)(2,1)} %get-tuple-element.10.high_ref, bf16[512,256]{1,0:T(8,128)(2,1)} %get-tuple-element.11.low_ref, f32[4,256,512]{2,1,0:T(8,128)} %get-tuple-element.12.white_ref, f32[1,2048,2048]{2,1,0:T(8,128)} %inverse_ref.3), custom_call_target="tpu_custom_call" | custom-call | flops 1610612736 | bytes 12582912 | tf_op jit(solution)/shard_map/update/pallas_call | solution.py:565
  73.7 0.0 copy-done
  73.7 0.8 %copy.18 = f32[1,8,16384]{2,1,0:T(8,128)} copy(f32[1,8,16384]{2,1,0:T(8,128)S(1)} %bitcast.13) | data formatting | bytes 1048576
Async XLA Ops:
  67.2 6.5 %copy-start = (f32[8,16384]{1,0:T(8,128)S(1)}, f32[8,16384]{1,0:T(8,128)}, u32[]{:S(2)}) copy-start(f32[8,16384]{1,0:T(8,128)} %get-tuple-element.8) | copy-start | bytes 1572868

commit v3 on v2

--- a/solution.py
+++ b/solution.py
@@ -32,8 +32,14 @@
     return dot(left_high, right_high) + (dot(left_high, right_low) + dot(left_low, right_high))
 
 
-def dot_terms(left, right):
-    return dot3(two_terms(left), two_terms(right), ((1,), (0,)))
+def dot_full(left, right, dims=((1,), (0,))):
+    return lax.dot_general(
+        left,
+        right,
+        dimension_numbers=(dims, ((), ())),
+        precision=lax.Precision.HIGHEST,
+        preferred_element_type=jnp.float32,
+    )
 
 
 def gather_kernel(
@@ -59,6 +65,8 @@
     work,
     block,
     block_rows,
+    spread_ref,
+    row_ref,
     load_sem,
     own_sem,
     a2a_send,
@@ -210,94 +218,6 @@
             device_id={"dev": dev, "rep": target},
         )
 
-    if low_count == 2:
-        for part in range(num_rep):
-            white_on(rep, part, 0, sibling).start()
-
-    partial[...] = dot3(
-        two_terms(rows[:, pl.ds(pl.multiple_of(rep * width, 128), width)]),
-        two_terms(white_ref[rep]),
-        ((1,), (1,)),
-    )
-
-    def group_rows(ref, owner):
-        return ref.at[pl.ds(pl.multiple_of(owner * group, 8), group)]
-
-    def sum_copy(step):
-        target = lax.rem(rep + step, num_rep)
-        return pltpu.make_async_remote_copy(
-            src_ref=group_rows(partial, target),
-            dst_ref=landed.at[step],
-            send_sem=sum_send.at[step],
-            recv_sem=sum_recv.at[step],
-            device_id={"dev": dev, "rep": target},
-        )
-
-    def share_copy(step):
-        piece = group_rows(cap, rep)
-        return pltpu.make_async_remote_copy(
-            src_ref=piece,
-            dst_ref=piece,
-            send_sem=share_send.at[step],
-            recv_sem=share_recv.at[step],
-            device_id={"dev": dev, "rep": lax.rem(rep + step, num_rep)},
-        )
-
-    for step in range(1, num_rep):
-        sum_copy(step).start()
-
-    diagonal = lax.broadcasted_iota(jnp.int32, (total, total), 0) == lax.broadcasted_iota(
-        jnp.int32, (total, total), 1
-    )
-    own_terms = jnp.sum(jnp.where(diagonal, partial[...], 0.0), axis=0, keepdims=True)
-    lev_dev[0] = jnp.broadcast_to(own_terms, (8, total))
-
-    def lev_copy(step):
-        return pltpu.make_async_remote_copy(
-            src_ref=lev_dev.at[0],
-            dst_ref=lev_dev.at[step],
-            send_sem=lev_send.at[step],
-            recv_sem=lev_recv.at[step],
-            device_id={"dev": lax.rem(dev + step, num_dev), "rep": rep},
-        )
-
-    def lev_start(step, carry):
-        lev_copy(step).start()
-        return carry
-
-    lax.fori_loop(1, num_dev, lev_start, 0)
-
-    total_rows = partial[pl.ds(pl.multiple_of(rep * group, 8), group), :]
-    for step in range(1, num_rep):
-        sum_copy(step).wait_recv()
-        total_rows = total_rows + landed[step]
-    cap[pl.ds(pl.multiple_of(rep * group, 8), group), :] = total_rows
-    for step in range(1, num_rep):
-        share_copy(step).start()
-
-    def lev_wait(step, carry):
-        lev_copy(step).wait_recv()
-        return carry
-
-    lax.fori_loop(1, num_dev, lev_wait, 0)
-    lev_rep[0] = jnp.sum(lev_dev[...], axis=0)
-
-    def lrep_copy(step):
-        return pltpu.make_async_remote_copy(
-            src_ref=lev_rep.at[0],
-            dst_ref=lev_rep.at[step],
-            send_sem=lrep_send.at[step],
-            recv_sem=lrep_recv.at[step],
-            device_id={"dev": dev, "rep": lax.rem(rep + step, num_rep)},
-        )
-
-    for step in range(1, num_rep):
-        lrep_copy(step).start()
-    for step in range(1, num_rep):
-        lrep_copy(step).wait_recv()
-    for step in range(1, num_rep):
-        share_copy(step).wait_recv()
-
     def part_order(target):
         if low_count == 2:
             first = target - lax.rem(target, 2)
@@ -307,12 +227,107 @@
             ]
         return [lax.rem(target + at, num_rep) for at in range(num_rep)]
 
-    for far in range(1, high_count):
-        for part in part_order(high_peer(far)):
-            white_on(rep, part, far, high_peer(far)).start()
-
+    early = min(2, num_rep)
+
+    def send_far(begin, end):
+        for far in range(1, high_count):
+            for part in part_order(high_peer(far))[begin:end]:
+                white_on(rep, part, far, high_peer(far)).start()
+
+    if low_count == 2:
+        for part in range(num_rep):
+            white_on(rep, part, 0, sibling).start()
+
+    partial[...] = dot3(
+        two_terms(rows[:, pl.ds(pl.multiple_of(rep * width, 128), width)]),
+        two_terms(white_ref[rep]),
+        ((1,), (1,)),
+    )
+
+    def group_rows(ref, owner):
+        return ref.at[pl.ds(pl.multiple_of(owner * group, 8), group)]
+
+    def sum_copy(step):
+        target = lax.rem(rep + step, num_rep)
+        return pltpu.make_async_remote_copy(
+            src_ref=group_rows(partial, target),
+            dst_ref=landed.at[step],
+            send_sem=sum_send.at[step],
+            recv_sem=sum_recv.at[step],
+            device_id={"dev": dev, "rep": target},
+        )
+
+    def share_copy(step):
+        piece = group_rows(cap, rep)
+        return pltpu.make_async_remote_copy(
+            src_ref=piece,
+            dst_ref=piece,
+            send_sem=share_send.at[step],
+            recv_sem=share_recv.at[step],
+            device_id={"dev": dev, "rep": lax.rem(rep + step, num_rep)},
+        )
+
+    for step in range(1, num_rep):
+        sum_copy(step).start()
+    send_far(0, 1)
+
+    diagonal = lax.broadcasted_iota(jnp.int32, (total, total), 0) == lax.broadcasted_iota(
+        jnp.int32, (total, total), 1
+    )
+    own_terms = jnp.sum(jnp.where(diagonal, partial[...], 0.0), axis=0, keepdims=True)
+    lev_dev[0] = jnp.broadcast_to(own_terms, (8, total))
+
+    def lev_copy(step):
+        return pltpu.make_async_remote_copy(
+            src_ref=lev_dev.at[0],
+            dst_ref=lev_dev.at[step],
+            send_sem=lev_send.at[step],
+            recv_sem=lev_recv.at[step],
+            device_id={"dev": lax.rem(dev + step, num_dev), "rep": rep},
+        )
+
+    def lev_start(step, carry):
+        lev_copy(step).start()
+        return carry
+
+    lax.fori_loop(1, num_dev, lev_start, 0)
+
+    total_rows = partial[pl.ds(pl.multiple_of(rep * group, 8), group), :]
+    for step in range(1, num_rep):
+        sum_copy(step).wait_recv()
+        total_rows = total_rows + landed[step]
+    cap[pl.ds(pl.multiple_of(rep * group, 8), group), :] = total_rows
+    for step in range(1, num_rep):
+        share_copy(step).start()
+    send_far(1, early)
+
+    def lev_wait(step, carry):
+        lev_copy(step).wait_recv()
+        return carry
+
+    lax.fori_loop(1, num_dev, lev_wait, 0)
+    lev_rep[0] = jnp.sum(lev_dev[...], axis=0)
+
+    def lrep_copy(step):
+        return pltpu.make_async_remote_copy(
+            src_ref=lev_rep.at[0],
+            dst_ref=lev_rep.at[step],
+            send_sem=lrep_send.at[step],
+            recv_sem=lrep_recv.at[step],
+            device_id={"dev": dev, "rep": lax.rem(rep + step, num_rep)},
+        )
+
+    for step in range(1, num_rep):
+        lrep_copy(step).start()
+    for step in range(1, num_rep):
+        lrep_copy(step).wait_recv()
+    for step in range(1, num_rep):
+        share_copy(step).wait_recv()
+
+    send_far(early, num_rep)
     leverage = jnp.sum(lev_rep[...], axis=0) / (num_dev * width * num_rep)
-    lev_ref[...] = leverage
+    own_first = rep * group + dev * examples
+    lev_ref[...] = pltpu.roll(leverage, total - own_first, 1)[0:1, 0:examples]
     damping = 1.0 + (width * num_rep) * leverage[0:1, :]
     work[...] = cap[...] + jnp.where(diagonal, damping, 0.0)
 
@@ -361,14 +376,13 @@
             if low_count == 2:
                 white_on(source, order[place], high_count + far, sibling).start()
 
-    early = min(2, num_rep)
     block_count = total // BLOCK
-    eliminate_blocks(0, block_count // 2, work, block, block_rows)
+    eliminate_blocks(0, block_count // 2, work, block, block_rows, spread_ref, row_ref)
     for far in range(1, high_count):
         pass_white(far, range(early))
         blocks.append((high_source(far), low_count * far))
         send_back(high_source(far), low_count * far)
-    eliminate_blocks(block_count // 2, block_count, work, block, block_rows)
+    eliminate_blocks(block_count // 2, block_count, work, block, block_rows, spread_ref, row_ref)
     for far in range(1, high_count):
         pass_white(far, range(early, num_rep))
     if low_count == 2:
@@ -379,7 +393,7 @@
             blocks.append((source, 2 * far + 1))
             send_back(source, 2 * far + 1)
 
-    solved = dot3(two_terms(white_ref[rep]), two_terms(work[...]), ((0,), (0,)))
+    solved = dot_full(white_ref[rep], work[...], ((0,), (0,)))
     high_part, low_part = two_terms(solved)
     high_ref[...] = high_part
     low_ref[...] = low_part
@@ -417,76 +431,114 @@
         share_copy(step).wait_send()
 
 
-def invert_block(block_ref):
+def sweep_pairs(entry):
+    def at(i, j):
+        return entry[min(i, j), max(i, j)]
+
+    for one in range(0, ROWS, 2):
+        two = one + 1
+        first, cross, second = at(one, one), at(one, two), at(two, two)
+        scale = 1.0 / (first * second - cross * cross)
+        p11, p12, p22 = second * scale, cross * scale, first * scale
+        rest = [i for i in range(ROWS) if i not in (one, two)]
+        scaled = {
+            i: (
+                at(i, one) * p11 - at(i, two) * p12,
+                at(i, two) * p22 - at(i, one) * p12,
+            )
+            for i in rest
+        }
+        for i in rest:
+            for j in rest:
+                if i <= j:
+                    entry[i, j] = entry[i, j] - (
+                        scaled[i][0] * at(j, one) + scaled[i][1] * at(j, two)
+                    )
+        for i in rest:
+            entry[min(i, one), max(i, one)] = scaled[i][0]
+            entry[min(i, two), max(i, two)] = scaled[i][1]
+        entry[one, one], entry[one, two], entry[two, two] = -p11, p12, -p22
+    return entry
+
+
+def invert_block(block_ref, spread_ref, row_ref):
     lane = lax.broadcasted_iota(jnp.int32, (ROWS, BLOCK), 1)
     row = lax.broadcasted_iota(jnp.int32, (ROWS, BLOCK), 0)
     lane_all = lax.broadcasted_iota(jnp.int32, (BLOCK, BLOCK), 1)
 
     def spread(value, col):
         return jnp.broadcast_to(value[:, col : col + 1], (ROWS, BLOCK))
+
+    def whole_row(ref, at):
+        return jnp.broadcast_to(ref[at : at + 1, :], (ROWS, BLOCK))
 
     for first in range(0, BLOCK, PANEL):
         panel = [block_ref[at : at + ROWS, :] for at in range(first, first + PANEL, ROWS)]
         for part in range(PANEL // ROWS):
             start = first + part * ROWS
-            pivots = panel[part]
-            columns = [spread(pivots, start + at) for at in range(ROWS)]
+            inside = (lane >= start) & (lane < start + ROWS)
+            for at in range(ROWS):
+                spread_ref[at * ROWS : (at + 1) * ROWS, :] = spread(panel[part], start + at)
+            row_ref[0:ROWS, :] = jnp.where(
+                inside, jnp.where(lane - start == row, 1.0, 0.0), panel[part]
+            )
             others = {
                 other: [spread(panel[other], start + at) for at in range(ROWS)]
                 for other in range(PANEL // ROWS)
                 if other != part
             }
+            entry = sweep_pairs(
+                {
+                    (i, j): whole_row(spread_ref, j * ROWS + i)
+                    for j in range(ROWS)
+                    for i in range(j + 1)
+                }
+            )
+            pivots = None
             for at in range(ROWS):
-                column = columns[at]
-                inverse_pivot = 1.0 / column[at : at + 1, :]
-                for later in range(at + 1, ROWS):
-                    scaled = columns[later][at : at + 1, :] * inverse_pivot
-                    columns[later] = jnp.where(
-                        row == at, scaled, columns[later] - column * scaled
-                    )
-                pivot_row = (
-                    jnp.where(lane[:1] == start + at, 1.0, pivots[at : at + 1, :])
-                    * inverse_pivot
-                )
-                pivots = jnp.where(
-                    row == at,
-                    pivot_row,
-                    jnp.where(lane == start + at, 0.0, pivots) - column * pivot_row,
-                )
+                column = entry[0, at]
+                for i in range(1, ROWS):
+                    column = jnp.where(row == i, entry[min(i, at), max(i, at)], column)
+                term = column * whole_row(row_ref, at)
+                pivots = -term if pivots is None else pivots - term
             panel[part] = pivots
+            row_ref[ROWS : 2 * ROWS, :] = pivots
             for other, spreads in others.items():
-                value = jnp.where((lane >= start) & (lane < start + ROWS), 0.0, panel[other])
+                value = jnp.where(inside, 0.0, panel[other])
                 for at in range(ROWS):
-                    value = value - spreads[at] * pivots[at : at + 1, :]
+                    value = value - spreads[at] * whole_row(row_ref, ROWS + at)
                 panel[other] = value
         panel = jnp.concatenate(panel, axis=0)
         whole = block_ref[...]
         inside = (lane_all >= first) & (lane_all < first + PANEL)
-        block_ref[...] = jnp.where(inside, 0.0, whole) - dot_terms(
+        block_ref[...] = jnp.where(inside, 0.0, whole) - dot_full(
             whole[:, first : first + PANEL], panel
         )
         block_ref[first : first + PANEL, :] = panel
 
 
-def eliminate_blocks(begin, end, cap, block, rows):
+def eliminate_blocks(begin, end, cap, block, rows, spread_ref, row_ref):
     total = cap.shape[0]
 
     def eliminate(at, carry):
         where = pl.ds(pl.multiple_of(at * BLOCK, BLOCK), BLOCK)
         block[...] = cap[where, where]
-        invert_block(block)
+        invert_block(block, spread_ref, row_ref)
         column = cap[:, where]
         cap[:, where] = jnp.zeros((total, BLOCK), jnp.float32)
-        rows[...] = dot_terms(block[...], cap[where, :])
+        rows[...] = dot_full(block[...], cap[where, :])
         rows[:, where] = block[...]
-        cap[...] = cap[...] - dot_terms(column, rows[...])
+        cap[...] = cap[...] - dot_full(column, rows[...])
         cap[where, :] = rows[...]
         return carry
 
     lax.fori_loop(begin, end, eliminate, 0)
 
 
-def update_kernel(rep_ref, high_ref, low_ref, white_ref, inverse_ref, out_ref):
+def update_kernel(
+    rep_ref, high_ref, low_ref, white_ref, inverse_ref, back_ref, out_ref, whitened_ref
+):
+    whitened_ref[0] = back_ref[...]
     out_ref[0] = inverse_ref[0] - dot3(
         (high_ref[...], low_ref[...]), two_terms(white_ref[0]), ((1,), (0,))
     )
@@ -511,14 +563,14 @@
     vmem = pl.BlockSpec(memory_space=pltpu.VMEM)
     hbm = pl.BlockSpec(memory_space=pl.ANY)
     dma = pltpu.SemaphoreType.DMA
-    all_white, solved_high, solved_low, all_lev, returned = pl.pallas_call(
+    all_white, solved_high, solved_low, lev_out, returned = pl.pallas_call(
         functools.partial(gather_kernel, num_dev, num_rep, examples),
         name="gather_whiten_solve",
         out_shape=(
             jax.ShapeDtypeStruct((num_rep, total, width), jnp.float32),
             jax.ShapeDtypeStruct((width, total), jnp.bfloat16),
             jax.ShapeDtypeStruct((width, total), jnp.bfloat16),
-            jax.ShapeDtypeStruct((8, total), jnp.float32),
+            jax.ShapeDtypeStruct((1, examples), jnp.float32),
             jax.ShapeDtypeStruct((examples, num_dev * feat_width), jnp.float32),
         ),
         in_specs=[vmem, hbm],
@@ -536,6 +588,8 @@
             pltpu.VMEM((total, total), jnp.float32),
             pltpu.VMEM((BLOCK, BLOCK), jnp.float32),
             pltpu.VMEM((BLOCK, total), jnp.float32),
+            pltpu.VMEM((ROWS * ROWS, BLOCK), jnp.float32),
+            pltpu.VMEM((2 * ROWS, BLOCK), jnp.float32),
             dma,
             dma,
             dma((num_dev,)),
@@ -562,7 +616,7 @@
     )(to_send, inverse)
 
     rep = lax.axis_index("rep")
-    updated = pl.pallas_call(
+    updated, whitened_out = pl.pallas_call(
         update_kernel,
         name="update",
         grid_spec=pltpu.PrefetchScalarGridSpec(
@@ -573,21 +627,26 @@
                 pl.BlockSpec((width, total), lambda c, r: (0, 0)),
                 pl.BlockSpec((1, total, width), lambda c, r: (c, 0, 0)),
                 pl.BlockSpec((1, width, width), lambda c, r: (0, r[0], c)),
+                pl.BlockSpec((examples, num_dev * width), lambda c, r: (0, c)),
             ],
-            out_specs=pl.BlockSpec((1, width, width), lambda c, r: (0, 0, c)),
+            out_specs=(
+                pl.BlockSpec((1, width, width), lambda c, r: (0, 0, c)),
+                pl.BlockSpec((1, examples, num_dev * width), lambda c, r: (0, 0, c)),
+            ),
         ),
-        out_shape=jax.ShapeDtypeStruct((1, width, feat_width), jnp.float32),
+        out_shape=(
+            jax.ShapeDtypeStruct((1, width, feat_width), jnp.float32),
+            jax.ShapeDtypeStruct((1, examples, num_dev * feat_width), jnp.float32),
+        ),
         compiler_params=pltpu.CompilerParams(vmem_limit_bytes=VMEM_BYTES),
         cost_estimate=pl.CostEstimate(
             flops=6 * total * width * feat_width,
             bytes_accessed=12 * width * feat_width,
             transcendentals=0,
         ),
-    )(jnp.reshape(rep, (1,)).astype(jnp.int32), solved_high, solved_low, all_white, inverse)
-
-    lev_first = rep * group_rows + lax.axis_index("dev") * examples
-    lev_out = lax.dynamic_slice_in_dim(all_lev[0], lev_first, examples, 0).reshape(1, examples)
-    return (returned.reshape(1, examples, num_dev * feat_width), lev_out, updated)
+    )(jnp.reshape(rep, (1,)).astype(jnp.int32), solved_high, solved_low, all_white, inverse, returned)
+
+    return (whitened_out, lev_out, updated)
 
 
 def solution(mesh):

time: 74.7 us -> 75.9 us (1.016)
  Pallas kernels: 67 us -> 69.7 us
  local copies, waits for them, and re-layouts: 6.42 us -> 4.86 us
    pallas_call x1, Pallas kernels: 60.5 us -> 62.9 us  [body(): pl.pallas_call(functools.partial(gather_kernel, num_dev, num_rep, example...]
where the time goes in v3:
time: 75.9 us; the launch traced here: 75.7 us
  Pallas kernels  69.7 us (92%)
  local copies, waits for them, and re-layouts  4.86 us (6%)
    pallas_call x1, Pallas kernels, body(): pl.pallas_call(functools.partial(gather_kernel, num_dev, num_rep, example...  62.9 us
    pallas_call x1, Pallas kernels, body(): pl.pallas_call(update_kernel, name='update', grid_spec=pltpu.PrefetchScal...  6.86 us
    unnamed x4, local copies, waits for them, and re-layouts  1.74 us
    reshape x1, local copies, waits for them, and re-layouts, body(): acts_four = activations.reshape(examples, tokens, num_dev, KI)  1.65 us

profile of v3, /device:TPU:0, one launch (start us, length us, event | category | flops | bytes accessed | tf_op | source)
XLA Modules:
  0.0 75.7 jit_solution(8188684383462212304)
XLA Ops:
  0.6 1.2 %copy.9 = bf16[1,8,64,256]{2,3,1,0:T(8,128)(2,1)S(1)} copy(bf16[1,8,64,256]{3,2,1,0:T(8,128)(2,1)} %param.4) | data formatting | bytes 524288 | tf_op args[1]
  1.9 1.6 %reshape.20 = bf16[8,64,8,64]{3,2,1,0:T(8,128)(2,1)S(1)} reshape(bf16[1,8,64,512]{3,2,1,0:T(8,128)(2,1)} %param.3) | data formatting | bytes 1048576 | tf_op jit(solution)/shard_map/reshape | solution.py:556
  3.5 0.4 convolution_multiply_fusion
  3.9 0.4 reshape.21
  4.3 1.1 %copy.16 = f32[8,8,2048]{2,0,1:T(8,128)} copy(f32[8,8,2048]{2,1,0:T(8,128)S(1)} %reshape.21) | data formatting | bytes 1048576 | tf_op jit(solution)/shard_map/mul | solution.py:561
  5.4 62.9 %gather_whiten_solve.1 = (f32[4,256,512]{2,1,0:T(8,128)}, bf16[512,256]{1,0:T(8,128)(2,1)}, bf16[512,256]{1,0:T(8,128)(2,1)}, f32[1,8]{1,0:T(1,128)}, f32[8,16384]{1,0:T(8,128)}) custom-call(f32[8,8,2048]{2,1,0:T(8,128)} %bitcast.10, f32[1,2048,2048]{2,1,0:T(8,128)} %inverse_ref.3), custom_call_target="tpu_custom_call" | custom-call | tf_op jit(solution)/shard_map/gather_whiten_solve/pallas_call | solution.py:566
  68.3 0.0 copy-start
  68.3 6.9 %update.1 = (f32[1,512,2048]{2,1,0:T(8,128)}, f32[1,8,16384]{2,1,0:T(8,128)}) custom-call(s32[1]{0:T(128)} %bitcast.rep_ref, bf16[512,256]{1,0:T(8,128)(2,1)} %get-tuple-element.10.high_ref, bf16[512,256]{1,0:T(8,128)(2,1)} %get-tuple-element.11.low_ref, f32[4,256,512]{2,1,0:T(8,128)} %get-tuple-element.12.white_ref, f32[1,2048,2048]{2,1,0:T(8,128)} %inverse_ref.3, ...), custom_call_target="tpu_custom_call" | custom-call | flops 1610612736 | bytes 12582912 | tf_op jit(solution)/shard_map/update/pallas_call | solution.py:619
  75.1 0.0 copy-done
  75.1 0.5 copy.18
Async XLA Ops:
  68.3 6.9 %copy-start = (f32[1,8]{1,0:T(1,128)S(1)}, f32[1,8]{1,0:T(1,128)}, u32[]{:S(2)}) copy-start(f32[1,8]{1,0:T(1,128)} %get-tuple-element.21) | copy-start | bytes 100

commit v4 on v3

--- a/solution.py
+++ b/solution.py
@@ -269,7 +269,6 @@
 
     for step in range(1, num_rep):
         sum_copy(step).start()
-    send_far(0, 1)
 
     diagonal = lax.broadcasted_iota(jnp.int32, (total, total), 0) == lax.broadcasted_iota(
         jnp.int32, (total, total), 1
@@ -299,7 +298,6 @@
     cap[pl.ds(pl.multiple_of(rep * group, 8), group), :] = total_rows
     for step in range(1, num_rep):
         share_copy(step).start()
-    send_far(1, early)
 
     def lev_wait(step, carry):
         lev_copy(step).wait_recv()
@@ -324,7 +322,7 @@
     for step in range(1, num_rep):
         share_copy(step).wait_recv()
 
-    send_far(early, num_rep)
+    send_far(0, num_rep)
     leverage = jnp.sum(lev_rep[...], axis=0) / (num_dev * width * num_rep)
     own_first = rep * group + dev * examples
     lev_ref[...] = pltpu.roll(leverage, total - own_first, 1)[0:1, 0:examples]
@@ -556,10 +554,9 @@
     acts_four = activations.reshape(examples, tokens, num_dev, KI)
     grads_four = out_grads.reshape(examples, tokens, num_dev, KO)
     features = jnp.einsum(
-        "etmo,etmi->emoi", grads_four, acts_four, preferred_element_type=jnp.float32
+        "etmo,etmi->meoi", grads_four, acts_four, preferred_element_type=jnp.float32
     )
-    features = features.reshape(examples, num_dev, feat_width) * tokens ** (-0.5)
-    to_send = features.transpose(1, 0, 2)
+    to_send = features.reshape(num_dev, examples, feat_width) * tokens ** (-0.5)
     vmem = pl.BlockSpec(memory_space=pltpu.VMEM)
     hbm = pl.BlockSpec(memory_space=pl.ANY)
     dma = pltpu.SemaphoreType.DMA

time: 75.9 us -> 73.1 us (0.963)
  Pallas kernels: 69.7 us -> 67.2 us
    pallas_call x1, Pallas kernels: 62.9 us -> 60.4 us  [body(): pl.pallas_call(functools.partial(gather_kernel, num_dev, num_rep, example...]
where the time goes in v4:
time: 73.1 us; the launch traced here: 72.9 us
  Pallas kernels  67.2 us (92%)
  local copies, waits for them, and re-layouts  4.55 us (6%)
    pallas_call x1, Pallas kernels, body(): pl.pallas_call(functools.partial(gather_kernel, num_dev, num_rep, example...  60.4 us
    pallas_call x1, Pallas kernels, body(): pl.pallas_call(update_kernel, name='update', grid_spec=pltpu.PrefetchScal...  6.86 us
    unnamed x4, local copies, waits for them, and re-layouts  1.74 us
    reshape x1, local copies, waits for them, and re-layouts, body(): acts_four = activations.reshape(examples, tokens, num_dev, KI)  1.65 us

profile of v4, /device:TPU:0, one launch (start us, length us, event | category | flops | bytes accessed | tf_op | source)
XLA Modules:
  0.0 72.9 jit_solution(9513730762473414372)
XLA Ops:
  0.6 1.2 %copy.8 = bf16[1,8,64,256]{2,3,1,0:T(8,128)(2,1)S(1)} copy(bf16[1,8,64,256]{3,2,1,0:T(8,128)(2,1)} %param.4) | data formatting | bytes 524288 | tf_op args[1]
  1.9 1.6 %reshape.20 = bf16[8,64,8,64]{3,2,1,0:T(8,128)(2,1)S(1)} reshape(bf16[1,8,64,512]{3,2,1,0:T(8,128)(2,1)} %param.3) | data formatting | bytes 1048576 | tf_op jit(solution)/shard_map/reshape | solution.py:554
  3.5 0.4 convolution_multiply_fusion
  3.9 1.2 %mul.10.send_ref = f32[8,8,2048]{2,1,0:T(8,128)} reshape(f32[8,8,32,64]{3,2,1,0:T(8,128)S(1)} %convolution_multiply_fusion) | data formatting | bytes 1048576 | tf_op jit(solution)/shard_map/mul | solution.py:559
  5.1 60.4 %gather_whiten_solve.1 = (f32[4,256,512]{2,1,0:T(8,128)}, bf16[512,256]{1,0:T(8,128)(2,1)}, bf16[512,256]{1,0:T(8,128)(2,1)}, f32[1,8]{1,0:T(1,128)}, f32[8,16384]{1,0:T(8,128)}) custom-call(f32[8,8,2048]{2,1,0:T(8,128)} %mul.10.send_ref, f32[1,2048,2048]{2,1,0:T(8,128)} %inverse_ref.3), custom_call_target="tpu_custom_call" | custom-call | tf_op jit(solution)/shard_map/gather_whiten_solve/pallas_call | solution.py:563
  65.5 0.0 copy-start
  65.5 6.9 %update.1 = (f32[1,512,2048]{2,1,0:T(8,128)}, f32[1,8,16384]{2,1,0:T(8,128)}) custom-call(s32[1]{0:T(128)} %bitcast.rep_ref, bf16[512,256]{1,0:T(8,128)(2,1)} %get-tuple-element.10.high_ref, bf16[512,256]{1,0:T(8,128)(2,1)} %get-tuple-element.11.low_ref, f32[4,256,512]{2,1,0:T(8,128)} %get-tuple-element.12.white_ref, f32[1,2048,2048]{2,1,0:T(8,128)} %inverse_ref.3, ...), custom_call_target="tpu_custom_call" | custom-call | flops 1610612736 | bytes 12582912 | tf_op jit(solution)/shard_map/update/pallas_call | solution.py:616
  72.3 0.0 copy-done
  72.3 0.5 copy.16
Async XLA Ops:
  65.5 6.9 %copy-start = (f32[1,8]{1,0:T(1,128)S(1)}, f32[1,8]{1,0:T(1,128)}, u32[]{:S(2)}) copy-start(f32[1,8]{1,0:T(1,128)} %get-tuple-element.21) | copy-start | bytes 100

commit v5 on v4

--- a/solution.py
+++ b/solution.py
@@ -381,20 +381,25 @@
         blocks.append((high_source(far), low_count * far))
         send_back(high_source(far), low_count * far)
     eliminate_blocks(block_count // 2, block_count, work, block, block_rows, spread_ref, row_ref)
-    for far in range(1, high_count):
-        pass_white(far, range(early, num_rep))
+    last = []
     if low_count == 2:
         for far in range(1, high_count):
             source = lax.rem(high + high_count - far, high_count) * 2 + (1 - low)
-            for part in range(num_rep):
-                white_on(source, part, high_count + far, rep).wait_recv()
+            white_on(source, rep, high_count + far, rep).wait_recv()
             blocks.append((source, 2 * far + 1))
             send_back(source, 2 * far + 1)
+            last.append((source, high_count + far))
+    for far in range(1, high_count):
+        pass_white(far, range(early, num_rep))
 
     solved = dot_full(white_ref[rep], work[...], ((0,), (0,)))
     high_part, low_part = two_terms(solved)
     high_ref[...] = high_part
     low_ref[...] = low_part
+
+    for source, kind in last:
+        for at in range(1, num_rep):
+            white_on(source, lax.rem(rep + at, num_rep), kind, rep).wait_recv()
 
     for column_block, slot in blocks:
 

time: 73.1 us -> 72.5 us (level)
  no operation moved by 1% of the time
where the time goes in v5:
time: 72.5 us; the launch traced here: 72.2 us
  Pallas kernels  66.6 us (92%)
  local copies, waits for them, and re-layouts  4.55 us (6%)
    pallas_call x1, Pallas kernels, body(): pl.pallas_call(functools.partial(gather_kernel, num_dev, num_rep, example...  59.8 us
    pallas_call x1, Pallas kernels, body(): pl.pallas_call(update_kernel, name='update', grid_spec=pltpu.PrefetchScal...  6.86 us
    unnamed x4, local copies, waits for them, and re-layouts  1.74 us
    reshape x1, local copies, waits for them, and re-layouts, body(): acts_four = activations.reshape(examples, tokens, num_dev, KI)  1.65 us

profile of v5, /device:TPU:0, one launch (start us, length us, event | category | flops | bytes accessed | tf_op | source)
XLA Modules:
  0.0 72.2 jit_solution(10111793142057230687)
XLA Ops:
  0.6 1.2 %copy.8 = bf16[1,8,64,256]{2,3,1,0:T(8,128)(2,1)S(1)} copy(bf16[1,8,64,256]{3,2,1,0:T(8,128)(2,1)} %param.4) | data formatting | bytes 524288 | tf_op args[1]
  1.9 1.6 %reshape.20 = bf16[8,64,8,64]{3,2,1,0:T(8,128)(2,1)S(1)} reshape(bf16[1,8,64,512]{3,2,1,0:T(8,128)(2,1)} %param.3) | data formatting | bytes 1048576 | tf_op jit(solution)/shard_map/reshape | solution.py:559
  3.5 0.4 convolution_multiply_fusion
  3.9 1.2 %mul.10.send_ref = f32[8,8,2048]{2,1,0:T(8,128)} reshape(f32[8,8,32,64]{3,2,1,0:T(8,128)S(1)} %convolution_multiply_fusion) | data formatting | bytes 1048576 | tf_op jit(solution)/shard_map/mul | solution.py:564
  5.1 59.8 %gather_whiten_solve.1 = (f32[4,256,512]{2,1,0:T(8,128)}, bf16[512,256]{1,0:T(8,128)(2,1)}, bf16[512,256]{1,0:T(8,128)(2,1)}, f32[1,8]{1,0:T(1,128)}, f32[8,16384]{1,0:T(8,128)}) custom-call(f32[8,8,2048]{2,1,0:T(8,128)} %mul.10.send_ref, f32[1,2048,2048]{2,1,0:T(8,128)} %inverse_ref.3), custom_call_target="tpu_custom_call" | custom-call | tf_op jit(solution)/shard_map/gather_whiten_solve/pallas_call | solution.py:568
  64.8 0.0 copy-start
  64.9 6.9 %update.1 = (f32[1,512,2048]{2,1,0:T(8,128)}, f32[1,8,16384]{2,1,0:T(8,128)}) custom-call(s32[1]{0:T(128)} %bitcast.rep_ref, bf16[512,256]{1,0:T(8,128)(2,1)} %get-tuple-element.10.high_ref, bf16[512,256]{1,0:T(8,128)(2,1)} %get-tuple-element.11.low_ref, f32[4,256,512]{2,1,0:T(8,128)} %get-tuple-element.12.white_ref, f32[1,2048,2048]{2,1,0:T(8,128)} %inverse_ref.3, ...), custom_call_target="tpu_custom_call" | custom-call | flops 1610612736 | bytes 12582912 | tf_op jit(solution)/shard_map/update/pallas_call | solution.py:621
  71.7 0.0 copy-done
  71.7 0.5 copy.16
Async XLA Ops:
  64.8 6.9 %copy-start = (f32[1,8]{1,0:T(1,128)S(1)}, f32[1,8]{1,0:T(1,128)}, u32[]{:S(2)}) copy-start(f32[1,8]{1,0:T(1,128)} %get-tuple-element.21) | copy-start | bytes 100
